TPU v7x, 256 devices: a whole 4x4x8 slice. The times are simulated.
256 devices in a mesh: ctx: 8 (over y, x_hi), dp: 16 (over x_lo, z), tp: 2 (over core).
Axes of the slice: x: 4 (x_hi: 2, x_lo: 2; x = x_hi * 2 + x_lo), y: 4, z: 8, core: 2. Of those that a mesh axis runs over, the one named last changes fastest.
Arguments:
- layer_input: bfloat16 [16, 2048, 8192], P('dp', 'ctx', 'tp'), may hold values from -6 to 6
- queries: bfloat16 [16, 2048, 4096], P('dp', 'ctx', 'tp'), may hold values from -64 to 64
- keys: bfloat16 [16, 2048, 512], P('dp', 'ctx', 'tp'), may hold values from -8 to 8
- values: bfloat16 [16, 2048, 512], P('dp', 'ctx', 'tp'), may hold values from -6 to 6
- out_grad: bfloat16 [16, 2048, 4096], P('dp', 'ctx', 'tp'), may hold values from -6 to 6
- doc_ids: int32 [16, 2048], P('dp', 'ctx'), may hold values from 0 to 3, never falling along the last dimension, each value on 1 to 1024 neighbouring positions
- freq_bins: int32 [64], replicated, may hold values from 0 to 32
- master: float32 [2, 4096, 512], P(None, 'dp', 'tp'), may hold values from -0.0625 to 0.0625
- moment1: float32 [2, 4096, 512], P(None, 'dp', 'tp'), may hold values from -3 to 3
- moment2: float32 [2, 4096, 512], P(None, 'dp', 'tp'), may hold values from 0.002 to 0.2
Outputs:
- query_grad: bfloat16 [16, 2048, 4096], P('dp', 'ctx', 'tp')
- value_grad: bfloat16 [16, 2048, 512], P('dp', 'ctx', 'tp')
- new_master: float32 [2, 4096, 512], P(None, 'dp', 'tp')
- new_moment1: float32 [2, 4096, 512], P(None, 'dp', 'tp')
- new_moment2: float32 [2, 4096, 512], P(None, 'dp', 'tp')
- key_weight: bfloat16 [2, 4096, 512], P(None, None, 'tp')
Inputs may be any that keep to these rules, and one draw needn't show every extreme that they name: `doc_ids`: each sequence holds 4 documents one after another, ids never falling along the sequence.
All inputs are finite; a program needn't handle non-finite values.
Results may differ from a plain program's by a relative error of at most 0.0079.
Values may be sent and summed in bfloat16 or wider, within the bound.
A program may use at most 128 MiB of HBM per device.

v0:
```python
import math
import jax
import jax.numpy as jnp
from jax import lax
from jax.sharding import PartitionSpec as P

HD = 128
BINS = 32
ADAM_STEP = 10
rope_base = 10000.0
yarn_factor = 8.0
magnitude_scale = 0.1 * math.log(8.0) + 1.0
beta_first = 0.9
beta_second = 0.95
adam_epsilon = 1e-08
learn_rate = 0.0003
weight_decay = 0.1


def frequencies(freq_bins):
    pairs = jnp.arange(HD // 2).astype(jnp.float32)
    theta = jnp.exp(pairs * (-2.0 * math.log(rope_base) / HD))
    gamma = freq_bins.astype(jnp.float32) / BINS
    return theta * ((1.0 - gamma) / yarn_factor + gamma)


def rotate(vectors, cosine, sine):
    half = vectors.shape[-1] // 2
    first = vectors[..., :half]
    second = vectors[..., half:]
    cosine = cosine[:, None, :]
    sine = sine[:, None, :]
    return jnp.concatenate(
        [first * cosine - second * sine, second * cosine + first * sine], axis=-1
    )


def unrotate(vectors, cosine, sine):
    half = vectors.shape[-1] // 2
    first = vectors[..., :half]
    second = vectors[..., half:]
    cosine = cosine[:, None, :]
    sine = sine[:, None, :]
    return jnp.concatenate(
        [first * cosine + second * sine, second * cosine - first * sine], axis=-1
    )


def on_device(
    layer_input, queries, keys, values, out_grad, doc_ids, freq_bins, master, moment1, moment2
):
    local_tokens = queries.shape[1]
    query_heads = queries.shape[2] // HD
    key_heads = keys.shape[2] // HD
    group_size = query_heads // key_heads
    ctx_count = lax.axis_size("ctx")
    data_count = lax.axis_size("dp")
    tp_count = lax.axis_size("tp")
    length = local_tokens * ctx_count
    inv_root = 1.0 / math.sqrt(HD)
    positions = lax.axis_index("ctx") * local_tokens + jnp.arange(local_tokens, dtype=jnp.int32)
    frequency = frequencies(freq_bins)
    angles = positions.astype(jnp.float32)[:, None] * frequency[None, :]
    cosine = jnp.cos(angles)
    sine = jnp.sin(angles)
    rot_q = (
        rotate(queries[0].reshape(local_tokens, query_heads, HD).astype(jnp.float32), cosine, sine)
        * magnitude_scale
    ).astype(jnp.bfloat16)
    rot_k = (
        rotate(keys[0].reshape(local_tokens, key_heads, HD).astype(jnp.float32), cosine, sine)
        * magnitude_scale
    ).astype(jnp.bfloat16)
    all_keys, all_values, all_docs = (
        lax.all_gather(rot_k.reshape(local_tokens, key_heads * HD), "ctx", axis=0, tiled=True),
        lax.all_gather(values[0], "ctx", axis=0, tiled=True),
        lax.all_gather(doc_ids[0], "ctx", axis=0, tiled=True),
    )
    key_positions = jnp.arange(length, dtype=jnp.int32)
    grad_heads = out_grad[0].reshape(local_tokens, query_heads, HD)
    query_rows = local_tokens * group_size
    block_rows = min(512, query_rows)
    block_count = query_rows // block_rows
    row_positions = jnp.repeat(positions, group_size).reshape(block_count, block_rows)
    row_docs = jnp.repeat(doc_ids[0], group_size).reshape(block_count, block_rows)
    contract_rows = (((0,), (0,)), ((), ()))
    query_parts = []
    key_parts = []
    value_parts = []
    for head in range(key_heads):
        query_block = rot_q[:, head * group_size : (head + 1) * group_size, :].reshape(
            block_count, block_rows, HD
        )
        grad_block = grad_heads[:, head * group_size : (head + 1) * group_size, :].reshape(
            block_count, block_rows, HD
        )
        key_head = all_keys[:, head * HD : (head + 1) * HD]
        value_head = all_values[:, head * HD : (head + 1) * HD]

        def one_block(carry, inputs):
            key_total, value_total = carry
            query_part, grad_part, pos_part, doc_part = inputs
            scores = (
                lax.dot_general(
                    query_part,
                    key_head,
                    (((1,), (1,)), ((), ())),
                    preferred_element_type=jnp.float32,
                )
                * inv_root
            )
            allowed = (key_positions[None, :] <= pos_part[:, None]) & (
                all_docs[None, :] == doc_part[:, None]
            )
            scores = jnp.where(allowed, scores, -jnp.inf)
            row_max = jnp.max(scores, axis=-1, keepdims=True)
            log_total = row_max + jnp.log(
                jnp.sum(jnp.exp(scores - row_max), axis=-1, keepdims=True)
            )
            probs = jnp.exp(scores - log_total)
            prob_grad = lax.dot_general(
                grad_part, value_head, (((1,), (1,)), ((), ())), preferred_element_type=jnp.float32
            )
            delta = jnp.sum(probs * prob_grad, axis=-1, keepdims=True)
            score_grad = (probs * (prob_grad - delta) * inv_root).astype(jnp.bfloat16)
            probs_bf = probs.astype(jnp.bfloat16)
            query_out = jnp.dot(score_grad, key_head, preferred_element_type=jnp.float32)
            key_total = key_total + lax.dot_general(
                score_grad, query_part, contract_rows, preferred_element_type=jnp.float32
            )
            value_total = value_total + lax.dot_general(
                probs_bf, grad_part, contract_rows, preferred_element_type=jnp.float32
            )
            return ((key_total, value_total), query_out)

        empty = jnp.zeros((length, HD), jnp.float32)
        (key_total, value_total), query_out = lax.scan(
            one_block, (empty, empty), (query_block, grad_block, row_positions, row_docs)
        )
        query_parts.append(query_out.reshape(local_tokens, group_size, HD))
        key_parts.append(key_total)
        value_parts.append(value_total)
    rot_q_grad = jnp.concatenate(query_parts, axis=1)
    key_terms = jnp.concatenate(key_parts, axis=1)
    value_terms = jnp.concatenate(value_parts, axis=1)
    key_sums, value_sums = (
        lax.psum_scatter(key_terms, "ctx", scatter_dimension=0, tiled=True),
        lax.psum_scatter(value_terms, "ctx", scatter_dimension=0, tiled=True),
    )
    query_grad = (
        (unrotate(rot_q_grad, cosine, sine) * magnitude_scale)
        .astype(jnp.bfloat16)
        .reshape(1, local_tokens, query_heads * HD)
    )
    value_grad = value_sums.astype(jnp.bfloat16).reshape(1, local_tokens, key_heads * HD)
    key_grad = (
        (unrotate(key_sums.reshape(local_tokens, key_heads, HD), cosine, sine) * magnitude_scale)
        .astype(jnp.bfloat16)
        .reshape(local_tokens, key_heads * HD)
    )
    gathered = lax.all_gather(layer_input[0], "tp", axis=1, tiled=True)
    group_rows = gathered.shape[1] // (tp_count * data_count)
    source = (
        gathered.reshape(local_tokens, tp_count, data_count, group_rows)
        .transpose(0, 2, 1, 3)
        .reshape(local_tokens, gathered.shape[1])
    )
    partial_sum = lax.psum_scatter(
        lax.dot_general(source, key_grad, contract_rows, preferred_element_type=jnp.float32),
        "dp",
        scatter_dimension=0,
        tiled=True,
    )
    gradient = lax.psum(partial_sum, "ctx")
    gradient = gradient * (1.0 / math.sqrt(data_count * length))
    gradient = gradient.reshape(tp_count, gradient.shape[0] // tp_count, gradient.shape[1])
    new_moment1 = beta_first * moment1 + (1.0 - beta_first) * gradient
    new_moment2 = beta_second * moment2 + (1.0 - beta_second) * gradient * gradient
    first_fix = 1.0 - beta_first**ADAM_STEP
    second_fix = 1.0 - beta_second**ADAM_STEP
    update = new_moment1 / first_fix / (jnp.sqrt(new_moment2 / second_fix) + adam_epsilon)
    new_master = master - learn_rate * (update + weight_decay * master)
    key_weight = lax.all_gather(new_master.astype(jnp.bfloat16), "dp", axis=1, tiled=True)
    return (query_grad, value_grad, new_master, new_moment1, new_moment2, key_weight)


def solution(mesh):
    placed = (
        P("dp", "ctx", "tp"),
        P("dp", "ctx", "tp"),
        P("dp", "ctx", "tp"),
        P("dp", "ctx", "tp"),
        P("dp", "ctx", "tp"),
        P("dp", "ctx"),
        P(),
        P(None, "dp", "tp"),
        P(None, "dp", "tp"),
        P(None, "dp", "tp"),
    )
    return jax.shard_map(
        on_device,
        mesh=mesh,
        in_specs=placed,
        out_specs=(
            P("dp", "ctx", "tp"),
            P("dp", "ctx", "tp"),
            P(None, "dp", "tp"),
            P(None, "dp", "tp"),
            P(None, "dp", "tp"),
            P(None, None, "tp"),
        ),
        check_vma=False,
    )
```

profile of v0, /device:TPU:8, one launch (start us, length us, event | category | flops | bytes accessed | tf_op | source)
XLA Modules:
  0.0 690.6 jit_solution(4289134766695654148)
XLA Ops:
  11.9 2.5 copy.22
  21.0 21.3 %all-gather = s32[1,2048]{1,0:T(1,128)S(1)} all-gather(s32[1,256]{1,0:T(1,128)S(1)} %copy-done.17), channel_id=2, replica_groups=mesh['ctx'=8,'dp'=16,'tp'=2] {'ctx'}, dimensions={1}, use_global_device_ids=true | all-gather | bytes 9216 | tf_op jit(solution)/shard_map/all_gather | solution.py:77
  43.8 20.8 %all-gather.12.cloned.1.call-done = bf16[1,2048,256]{2,1,0:T(8,128)(2,1)} async-done(((bf16[1,256,256]{2,1,0:T(8,128)(2,1)}), bf16[1,2048,256]{2,1,0:T(8,128)(2,1)}) %all-gather.12.cloned.1.call-update) | async-done | bytes 1048592 | tf_op jit(solution)/shard_map/all_gather | solution.py:76
  64.7 2.1 fusion.51
  66.8 51.4 %all-gather.8.cloned.1.call-done = bf16[2048,256]{1,0:T(8,128)(2,1)} async-done(((bf16[256,256]{1,0:T(8,128)(2,1)}), bf16[2048,256]{1,0:T(8,128)(2,1)}) %all-gather.8.cloned.1.call-update) | async-done | bytes 1048592 | tf_op jit(solution)/shard_map/all_gather | solution.py:75
  118.2 2.1 fusion.53
  121.3 54.4 %while.30 = (s32[]{:T(128)}, f32[2048,128]{1,0:T(8,128)}, f32[2048,128]{1,0:T(8,128)}, f32[4,512,128]{2,1,0:T(8,128)}, s32[4,512]{1,0:T(4,128)S(1)}, /*index=5*/...) while((s32[]{:T(128)}, f32[2048,128]{1,0:T(8,128)}, ...), condition=%wide.region_4.5_spmd.clone, body=%wide.region_0.4_spmd.clone.sunk | while | flops 1362099200 | bytes 92581816 | solution.py:137
  125.7 2.9 convolution_add_fusion.8
  128.5 2.5 fusion.95
  131.0 3.2 convolution_add_fusion.9
  138.8 3.3 convolution_add_fusion.8
  142.0 2.5 fusion.95
  144.5 3.6 convolution_add_fusion.9
  152.6 3.3 convolution_add_fusion.8
  155.8 2.4 fusion.95
  158.3 3.6 convolution_add_fusion.9
  166.4 3.3 convolution_add_fusion.8
  169.6 2.5 fusion.95
  172.1 3.6 convolution_add_fusion.9
  176.8 59.3 %while.31 = (s32[]{:T(128)}, f32[2048,128]{1,0:T(8,128)S(1)}, f32[2048,128]{1,0:T(8,128)}, f32[4,512,128]{2,1,0:T(8,128)}, s32[4,512]{1,0:T(4,128)S(1)}, /*index...) while((s32[]{:T(128)}, f32[2048,128]{1,0:T(8,128)S(1)}, ...), condition=%wide.region_9.10_spmd.clone, body=%wide.region_5.9_spmd.clone.sunk | while | flops 1362099200 | bytes 77902560 | solution.py:137
  176.8 2.4 fusion.104
  183.7 2.1 convolution_add_fusion.10
  185.8 2.5 fusion.105
  188.3 3.0 convolution_add_fusion.11
  191.3 2.4 fusion.104
  198.2 2.1 convolution_add_fusion.10
  200.3 2.5 fusion.105
  202.8 3.4 convolution_add_fusion.11
  206.2 2.4 fusion.104
  210.0 2.0 multiply_reduce_fusion.5
  213.1 2.1 convolution_add_fusion.10
  215.3 2.5 fusion.105
  217.7 3.4 convolution_add_fusion.11
  221.2 2.4 fusion.104
  228.1 2.1 convolution_add_fusion.10
  230.2 2.5 fusion.105
  232.7 3.4 convolution_add_fusion.11
  236.1 2.8 pad_maximum_fusion.2
  238.9 4.6 copy.23
  243.6 74.3 %reduce-scatter.6.cloned.1.call-done = f32[256,256]{1,0:T(8,128)} async-done(((f32[2048,256]{1,0:T(8,128)}), f32[256,256]{1,0:T(8,128)}) %reduce-scatter.6.cloned.1.call-update) | async-done | bytes 262160 | tf_op jit(solution)/shard_map/reduce_scatter | solution.py:147
  319.9 6.8 convolution_bitcast_fusion.2
  326.7 100.4 %reduce-scatter.8.cloned.1.call-done = f32[512,256]{0,1:T(8,128)} async-done(((f32[8192,256]{0,1:T(8,128)}), f32[512,256]{0,1:T(8,128)}) %reduce-scatter.8.cloned.1.call-update) | async-done | bytes 524304 | tf_op jit(solution)/shard_map/reduce_scatter | solution.py:168
  427.2 3.0 pad_maximum_fusion.1
  430.3 86.8 %all-reduce.2.cloned.1.call-done = f32[512,256]{0,1:T(8,128)} async-done(((f32[512,256]{0,1:T(8,128)}), f32[512,256]{0,1:T(8,128)}) %all-reduce.2.cloned.1.call-update) | async-done | bytes 524304 | tf_op jit(solution)/shard_map/psum | solution.py:174
  518.4 3.0 fusion.47
  524.2 77.1 %reduce-scatter.4.cloned.1.call-done = f32[256,256]{1,0:T(8,128)} async-done(((f32[2048,256]{1,0:T(8,128)}), f32[256,256]{1,0:T(8,128)}) %reduce-scatter.4.cloned.1.call-update) | async-done | bytes 262160 | tf_op jit(solution)/shard_map/reduce_scatter | solution.py:148
  602.9 76.4 %all-gather.10.cloned.1.call-done = bf16[2,4096,256]{2,1,0:T(8,128)(2,1)} async-done(((bf16[2,256,256]{2,1,0:T(8,128)(2,1)}), bf16[2,4096,256]{2,1,0:T(8,128)(2,1)}) %all-gather.10.cloned.1.call-update) | async-done | bytes 4194320 | tf_op jit(solution)/shard_map/all_gather | solution.py:183
  679.3 4.5 copy.66
  (211 shorter events, 56.2 us)
Async XLA Ops:
  7.2 4.7 copy-start.15
  7.2 57.5 %all-gather.12.cloned.1.call-start = ((), (), s32[]{:S(2)}) async-start(), calls=%async_computation.9 | async-start | bytes 1179648 | tf_op jit(solution)/shard_map/all_gather | solution.py:76
  7.9 110.2 %all-gather.8.cloned.1.call-start = ((), (), s32[]{:S(2)}) async-start(), calls=%async_computation.3 | async-start | bytes 1179648 | tf_op jit(solution)/shard_map/all_gather | solution.py:75
  11.8 227.1 %all-gather.14.cloned.1.call-start = ((), (), s32[]{:S(2)}) async-start(), calls=%async_computation.10 | async-start | bytes 6291456 | tf_op jit(solution)/shard_map/all_gather | solution.py:161
  14.4 303.5 %reduce-scatter.6.cloned.1.call-start = ((), (), s32[]{:S(2)}) async-start(), calls=%async_computation.5 | async-start | bytes 2359296 | tf_op jit(solution)/shard_map/reduce_scatter | solution.py:147
  18.6 2.3 copy-start.17
  121.3 2.0 copy-start.5
  121.3 2.0 copy-start.9
  125.7 5.4 copy-start.1
  131.0 3.3 copy-start.6
  131.0 3.3 copy-start.8
  131.0 3.3 copy-start.10
  131.0 3.3 copy-start.14
  134.3 2.0 copy-start.5
  134.3 2.0 copy-start.9
  138.7 5.7 copy-start.1
  144.5 3.6 copy-start.6
  144.5 3.6 copy-start.8
  144.5 3.6 copy-start.10
  144.5 3.6 copy-start.14
  148.1 2.0 copy-start.5
  148.1 2.0 copy-start.9
  152.5 5.7 copy-start.1
  158.3 3.6 copy-start.6
  158.3 3.6 copy-start.8
  158.3 3.6 copy-start.10
  158.3 3.6 copy-start.14
  161.9 2.0 copy-start.5
  161.9 2.0 copy-start.9
  166.3 5.7 copy-start.1
  172.1 3.6 copy-start.6
  172.1 3.6 copy-start.8
  172.1 3.6 copy-start.10
  172.1 3.6 copy-start.14
  179.1 3.5 copy-start.2
  183.7 4.6 copy-start.3
  193.7 3.5 copy-start.2
  198.2 4.6 copy-start.3
  208.6 3.5 copy-start.2
  213.1 4.6 copy-start.3
  223.5 3.5 copy-start.2
  228.1 4.6 copy-start.3
  238.9 188.3 %reduce-scatter.8.cloned.1.call-start = ((), (), s32[]{:S(2)}) async-start(), calls=%async_computation.6 | async-start | bytes 8912896 | tf_op jit(solution)/shard_map/reduce_scatter | solution.py:168
  326.7 190.4 %all-reduce.2.cloned.1.call-start = ((), (), s32[]{:S(2)}) async-start(), calls=%async_computation.7 | async-start | bytes 1048576 | tf_op jit(solution)/shard_map/psum | solution.py:174
  427.2 174.1 %reduce-scatter.4.cloned.1.call-start = ((), (), s32[]{:S(2)}) async-start(), calls=%async_computation.4 | async-start | bytes 2359296 | tf_op jit(solution)/shard_map/reduce_scatter | solution.py:148
  430.2 249.1 %all-gather.10.cloned.1.call-start = ((), (), s32[]{:S(2)}) async-start(), calls=%async_computation.8 | async-start | bytes 4456448 | tf_op jit(solution)/shard_map/all_gather | solution.py:183
  518.4 3.0 copy-start.11
  518.4 3.0 copy-start.12
  (17 other events, 25.4 us)
Sparse Core Ops, SparseCore 0:
  10.7 53.9 all-gather.11
  67.9 50.2 all-gather.7
  120.0 18.1 all-gather.13
  239.0 78.8 reduce-scatter.5
  326.8 100.2 reduce-scatter.7
  429.6 87.4 all-reduce.1
  522.2 79.0 reduce-scatter.3
  603.2 76.0 all-gather.9
where the time goes:
time: 692 us; the launch traced here: 691 us
  waiting for transfers between devices  488 us (71%)
  matrix products  101 us (15%)
  other arithmetic  32.4 us (5%)
  local copies, waits for them, and re-layouts  31.9 us (5%)
  blocking collectives  21.3 us (3%)
  between operations  14.4 us (2%)
    reduce_scatter x1, waiting for transfers between devices, on_device(): lax.psum_scatter(lax.dot_general(source, key_grad, contract_rows, preferr...  100 us
    psum x1, waiting for transfers between devices, on_device(): gradient = lax.psum(partial_sum, 'ctx')  86.8 us
    reduce_scatter x1, waiting for transfers between devices, on_device(): lax.psum_scatter(value_terms, 'ctx', scatter_dimension=0, tiled=True)  77.1 us
    all_gather x1, waiting for transfers between devices, on_device(): lax.all_gather(new_master.astype(jnp.bfloat16), 'dp', axis=1, tiled=True)  76.4 us
    reduce_scatter x1, waiting for transfers between devices, on_device(): lax.psum_scatter(key_terms, 'ctx', scatter_dimension=0, tiled=True)  74.3 us
    all_gather x1, waiting for transfers between devices, on_device(): lax.all_gather(rot_k.reshape(local_tokens, key_heads * HD), 'ctx', axis=0...  51.4 us
    dot_general x8, matrix products, one_block(): lax.dot_general(probs_bf, grad_part, contract_rows, preferred_element_typ...  27.3 us
    all_gather x1, blocking collectives, on_device(): lax.all_gather(doc_ids[0], 'ctx', axis=0, tiled=True)  21.3 us
  transfers between devices with their start and end apart: 8, of which 7 were waited for; matrix products, arithmetic and copies ran while one was open for 21% of the time, Pallas kernels for 0%

commit v1 on v0

--- a/solution.py
+++ b/solution.py
@@ -72,7 +72,15 @@
         * magnitude_scale
     ).astype(jnp.bfloat16)
     all_keys, all_values, all_docs = (
-        lax.all_gather(rot_k.reshape(local_tokens, key_heads * HD), "ctx", axis=0, tiled=True),
+        jnp.concatenate(
+            lax.all_to_all(
+                jnp.stack([rot_k.reshape(local_tokens, key_heads * HD)] * lax.axis_size("ctx")),
+                "ctx",
+                0,
+                0,
+            ),
+            axis=0,
+        ),
         lax.all_gather(values[0], "ctx", axis=0, tiled=True),
         lax.all_gather(doc_ids[0], "ctx", axis=0, tiled=True),
     )

time: 692 us -> 641 us (0.926)
  waiting for transfers between devices: 488 us -> 428 us
  starting transfers between devices: 0.32 us -> 7.62 us
    all_gather x1 -> x0, waiting for transfers between devices: 51.4 us -> none  [on_device(): lax.all_gather(rot_k.reshape(local_tokens, key_heads * HD), 'ctx', axis=0...]
    all_gather x1, waiting for transfers between devices: 20.8 us -> 12.2 us  [on_device(): lax.all_gather(values[0], 'ctx', axis=0, tiled=True)]
    all_to_all x0 -> x1, starting transfers between devices: none -> 7.38 us  [on_device(): lax.all_to_all(jnp.stack([rot_k.reshape(local_tokens, key_heads * HD)] *...]
  transfers between devices with their start and end apart: 8 -> 8, of which waited for: 7 -> 6; matrix products, arithmetic and copies ran while one was open for 21% -> 23% of each run, Pallas kernels for 0% -> 0%
where the time goes in v1:
time: 641 us; the launch traced here: 639 us
  waiting for transfers between devices  428 us (67%)
  matrix products  101 us (16%)
  local copies, waits for them, and re-layouts  33.8 us (5%)
  other arithmetic  32.4 us (5%)
  blocking collectives  21.2 us (3%)
  between operations  14.4 us (2%)
  starting transfers between devices  7.62 us (1%)
    reduce_scatter x1, waiting for transfers between devices, on_device(): lax.psum_scatter(lax.dot_general(source, key_grad, contract_rows, preferr...  100 us
    psum x1, waiting for transfers between devices, on_device(): gradient = lax.psum(partial_sum, 'ctx')  86.8 us
    reduce_scatter x1, waiting for transfers between devices, on_device(): lax.psum_scatter(value_terms, 'ctx', scatter_dimension=0, tiled=True)  76.9 us
    all_gather x1, waiting for transfers between devices, on_device(): lax.all_gather(new_master.astype(jnp.bfloat16), 'dp', axis=1, tiled=True)  76.4 us
    reduce_scatter x1, waiting for transfers between devices, on_device(): lax.psum_scatter(key_terms, 'ctx', scatter_dimension=0, tiled=True)  74.3 us
    dot_general x8, matrix products, one_block(): lax.dot_general(probs_bf, grad_part, contract_rows, preferred_element_typ...  27.3 us
    all_gather x1, blocking collectives, on_device(): lax.all_gather(doc_ids[0], 'ctx', axis=0, tiled=True)  21.2 us
    dot_general x8, matrix products, one_block(): lax.dot_general(score_grad, query_part, contract_rows, preferred_element_...  21 us
  transfers between devices with their start and end apart: 8, of which 6 were waited for; matrix products, arithmetic and copies ran while one was open for 23% of the time, Pallas kernels for 0%

profile of v1, /device:TPU:8, one launch (start us, length us, event | category | flops | bytes accessed | tf_op | source)
XLA Modules:
  0.0 639.3 jit_solution(1445516125438166966)
XLA Ops:
  12.2 7.4 %all-to-all-start = ((bf16[8,256,256]{2,1,0:T(8,128)(2,1)}), bf16[8,256,256]{2,1,0:T(8,128)(2,1)}, u32[]{:S(2)}, u32[]{:S(2)}) async-start(bf16[8,256,256]{2,1,0:T(8,128)(2,1)} %stack.3), calls=%async_computation | async-start | bytes 2097152 | tf_op jit(solution)/shard_map/all_to_all | solution.py:76
  19.5 2.5 copy.22
  24.1 2.4 copy.30
  26.5 21.2 %all-gather = s32[1,2048]{1,0:T(1,128)} all-gather(s32[1,256]{1,0:T(1,128)S(1)} %copy-done.19), channel_id=2, replica_groups=mesh['ctx'=8,'dp'=16,'tp'=2] {'ctx'}, dimensions={1}, use_global_device_ids=true | all-gather | bytes 9216 | tf_op jit(solution)/shard_map/all_gather | solution.py:85
  52.8 2.1 fusion.53
  54.9 12.2 %all-gather.9.cloned.1.call-done = bf16[1,2048,256]{2,1,0:T(8,128)(2,1)} async-done(((bf16[1,256,256]{2,1,0:T(8,128)(2,1)}), bf16[1,2048,256]{2,1,0:T(8,128)(2,1)}) %all-gather.9.cloned.1.call-update) | async-done | bytes 1048592 | tf_op jit(solution)/shard_map/all_gather | solution.py:84
  67.1 2.1 fusion.51
  70.2 54.4 %while.30 = (s32[]{:T(128)}, f32[2048,128]{1,0:T(8,128)}, f32[2048,128]{1,0:T(8,128)}, f32[4,512,128]{2,1,0:T(8,128)}, s32[4,512]{1,0:T(4,128)S(1)}, /*index=5*/...) while((s32[]{:T(128)}, f32[2048,128]{1,0:T(8,128)}, ...), condition=%wide.region_4.5_spmd.clone, body=%wide.region_0.4_spmd.clone.sunk | while | flops 1362099200 | bytes 92581816 | solution.py:145
  74.6 2.9 convolution_add_fusion.8
  77.5 2.5 fusion.95
  80.0 3.2 convolution_add_fusion.9
  87.7 3.3 convolution_add_fusion.8
  90.9 2.5 fusion.95
  93.4 3.6 convolution_add_fusion.9
  101.5 3.3 convolution_add_fusion.8
  104.7 2.4 fusion.95
  107.2 3.6 convolution_add_fusion.9
  115.3 3.3 convolution_add_fusion.8
  118.5 2.5 fusion.95
  121.0 3.6 convolution_add_fusion.9
  125.7 59.3 %while.31 = (s32[]{:T(128)}, f32[2048,128]{1,0:T(8,128)S(1)}, f32[2048,128]{1,0:T(8,128)}, f32[4,512,128]{2,1,0:T(8,128)}, s32[4,512]{1,0:T(4,128)S(1)}, /*index...) while((s32[]{:T(128)}, f32[2048,128]{1,0:T(8,128)S(1)}, ...), condition=%wide.region_9.10_spmd.clone, body=%wide.region_5.9_spmd.clone.sunk | while | flops 1362099200 | bytes 77902560 | solution.py:145
  125.7 2.4 fusion.104
  132.6 2.1 convolution_add_fusion.10
  134.7 2.5 fusion.105
  137.2 3.0 convolution_add_fusion.11
  140.2 2.4 fusion.104
  147.2 2.1 convolution_add_fusion.10
  149.3 2.5 fusion.105
  151.7 3.4 convolution_add_fusion.11
  155.2 2.4 fusion.104
  162.1 2.1 convolution_add_fusion.10
  164.2 2.5 fusion.105
  166.7 3.4 convolution_add_fusion.11
  170.1 2.4 fusion.104
  177.0 2.1 convolution_add_fusion.10
  179.1 2.5 fusion.105
  181.6 3.4 convolution_add_fusion.11
  185.0 2.8 pad_maximum_fusion.2
  187.9 4.6 copy.23
  192.5 74.3 %reduce-scatter.6.cloned.1.call-done = f32[256,256]{1,0:T(8,128)} async-done(((f32[2048,256]{1,0:T(8,128)}), f32[256,256]{1,0:T(8,128)}) %reduce-scatter.6.cloned.1.call-update) | async-done | bytes 262160 | tf_op jit(solution)/shard_map/reduce_scatter | solution.py:155
  268.8 6.8 %convolution_bitcast_fusion.2 = f32[8192,256]{0,1:T(8,128)} fusion(bf16[256,8192]{0,1:T(8,128)(2,1)} %bitcast.133, bf16[32,8,2,128]{3,2,1,0:T(2,128)(2,1)S(1)} %bitcast.145), kind=kOutput, calls=%fused_computation.60 | convolution fusion | flops 1073741824 | bytes 12713984 | tf_op jit(solution)/shard_map/dot_general | solution.py:177
  275.7 100.4 %reduce-scatter.8.cloned.1.call-done = f32[512,256]{0,1:T(8,128)} async-done(((f32[8192,256]{0,1:T(8,128)}), f32[512,256]{0,1:T(8,128)}) %reduce-scatter.8.cloned.1.call-update) | async-done | bytes 524304 | tf_op jit(solution)/shard_map/reduce_scatter | solution.py:176
  376.2 3.0 pad_maximum_fusion.1
  379.3 86.8 %all-reduce.2.cloned.1.call-done = f32[512,256]{0,1:T(8,128)} async-done(((f32[512,256]{0,1:T(8,128)}), f32[512,256]{0,1:T(8,128)}) %all-reduce.2.cloned.1.call-update) | async-done | bytes 524304 | tf_op jit(solution)/shard_map/psum | solution.py:182
  467.3 3.0 fusion.47
  473.1 76.9 %reduce-scatter.4.cloned.1.call-done = f32[256,256]{1,0:T(8,128)} async-done(((f32[2048,256]{1,0:T(8,128)}), f32[256,256]{1,0:T(8,128)}) %reduce-scatter.4.cloned.1.call-update) | async-done | bytes 262160 | tf_op jit(solution)/shard_map/reduce_scatter | solution.py:156
  551.6 76.4 %all-gather.7.cloned.1.call-done = bf16[2,4096,256]{2,1,0:T(8,128)(2,1)} async-done(((bf16[2,256,256]{2,1,0:T(8,128)(2,1)}), bf16[2,4096,256]{2,1,0:T(8,128)(2,1)}) %all-gather.7.cloned.1.call-update) | async-done | bytes 4194320 | tf_op jit(solution)/shard_map/all_gather | solution.py:191
  628.0 4.5 copy.66
  (215 shorter events, 57.5 us)
Async XLA Ops:
  7.2 59.9 %all-gather.9.cloned.1.call-start = ((), (), s32[]{:S(2)}) async-start(), calls=%async_computation.9 | async-start | bytes 1179648 | tf_op jit(solution)/shard_map/all_gather | solution.py:84
  10.7 8.8 %copy-start.16 = (bf16[1,256,4096]{2,1,0:T(8,128)(2,1)S(1)}, bf16[1,256,4096]{2,1,0:T(8,128)(2,1)}, u32[]{:S(2)}) copy-start(bf16[1,256,4096]{2,1,0:T(8,128)(2,1)} %param.14) | copy-start | bytes 6291460
  12.2 40.7 %all-to-all-start = ((bf16[8,256,256]{2,1,0:T(8,128)(2,1)}), bf16[8,256,256]{2,1,0:T(8,128)(2,1)}, u32[]{:S(2)}, u32[]{:S(2)}) async-start(bf16[8,256,256]{2,1,0:T(8,128)(2,1)} %stack.3), calls=%async_computation | async-start | bytes 2097152 | tf_op jit(solution)/shard_map/all_to_all | solution.py:76
  19.5 168.3 %all-gather.11.cloned.1.call-start = ((), (), s32[]{:S(2)}) async-start(), calls=%async_computation.10 | async-start | bytes 6291456 | tf_op jit(solution)/shard_map/all_gather | solution.py:169
  22.0 244.8 %reduce-scatter.6.cloned.1.call-start = ((), (), s32[]{:S(2)}) async-start(), calls=%async_computation.5 | async-start | bytes 2359296 | tf_op jit(solution)/shard_map/reduce_scatter | solution.py:155
  23.9 2.7 copy-start.19
  54.9 15.3 %copy-start.18 = (s32[1,2048]{1,0:T(1,128)S(1)}, s32[1,2048]{1,0:T(1,128)}, u32[]{:S(2)}) copy-start(s32[1,2048]{1,0:T(1,128)} %all-gather) | copy-start | bytes 24580
  70.2 2.0 copy-start.9
  74.6 5.4 copy-start.1
  80.0 3.3 copy-start.6
  80.0 3.3 copy-start.8
  80.0 3.3 copy-start.10
  80.0 3.3 copy-start.15
  83.3 2.0 copy-start.5
  83.3 2.0 copy-start.9
  87.7 5.7 copy-start.1
  93.4 3.6 copy-start.6
  93.4 3.6 copy-start.8
  93.4 3.6 copy-start.10
  93.4 3.6 copy-start.15
  97.1 2.0 copy-start.5
  97.1 2.0 copy-start.9
  101.5 5.7 copy-start.1
  107.2 3.6 copy-start.6
  107.2 3.6 copy-start.8
  107.2 3.6 copy-start.10
  107.2 3.6 copy-start.15
  110.8 2.0 copy-start.5
  110.9 2.0 copy-start.9
  115.3 5.7 copy-start.1
  121.0 3.6 copy-start.6
  121.0 3.6 copy-start.8
  121.0 3.6 copy-start.10
  121.0 3.6 copy-start.15
  128.1 3.5 copy-start.2
  132.6 4.6 copy-start.3
  142.6 3.5 copy-start.2
  147.1 4.6 copy-start.3
  157.5 3.5 copy-start.2
  162.1 4.6 copy-start.3
  172.5 3.5 copy-start.2
  177.0 4.6 copy-start.3
  187.8 188.3 %reduce-scatter.8.cloned.1.call-start = ((), (), s32[]{:S(2)}) async-start(), calls=%async_computation.6 | async-start | bytes 8912896 | tf_op jit(solution)/shard_map/reduce_scatter | solution.py:176
  275.7 190.3 %all-reduce.2.cloned.1.call-start = ((), (), s32[]{:S(2)}) async-start(), calls=%async_computation.7 | async-start | bytes 1048576 | tf_op jit(solution)/shard_map/psum | solution.py:182
  376.1 173.9 %reduce-scatter.4.cloned.1.call-start = ((), (), s32[]{:S(2)}) async-start(), calls=%async_computation.4 | async-start | bytes 2359296 | tf_op jit(solution)/shard_map/reduce_scatter | solution.py:156
  379.2 248.8 %all-gather.7.cloned.1.call-start = ((), (), s32[]{:S(2)}) async-start(), calls=%async_computation.8 | async-start | bytes 4456448 | tf_op jit(solution)/shard_map/all_gather | solution.py:191
  467.3 3.0 copy-start.11
  467.3 3.0 copy-start.12
  (19 other events, 28.8 us)
Sparse Core Ops, SparseCore 0:
  10.6 56.3 all-gather.8
  68.9 18.1 all-gather.10
  187.9 78.8 reduce-scatter.5
  275.8 100.2 reduce-scatter.7
  378.6 87.3 all-reduce.1
  471.0 78.9 reduce-scatter.3
  551.9 76.0 all-gather.6
